TPU v7x, 32 devices: a whole 2x2x4 slice. The times are simulated.
32 devices in a mesh: dp: 4 (over y, x), head: 8 (over z, core).
Axes of the slice: x: 2, y: 2, z: 4, core: 2. Of those that a mesh axis runs over, the one named last changes fastest.
Arguments:
- query: bfloat16 [4096, 12288], P(('dp', 'head')), may hold values from -160 to 160
- latent: bfloat16 [4096, 576], P(('dp', 'head')), may hold values from -6 to 6
- d_attn: bfloat16 [4096, 8192], P(('dp', 'head')), may hold values from -6 to 6
- w_kv: bfloat16 [512, 16384], P('dp', 'head'), may hold values from -0.25 to 0.25
- doc_lengths: int32 [4, 5], P('dp'), may hold values from 1 to 384, 1024 in all within a row
Outputs:
- d_query: bfloat16 [4096, 12288], P(('dp', 'head'))
- d_latent: float32 [4096, 576], P(('dp', 'head'))
- d_w_kv: float32 [512, 16384], P('dp', 'head')
Inputs may be any that keep to these rules, and one draw needn't show every extreme that they name: `doc_lengths`: row g lists the lengths of the 5 documents of data group g; they sum to 1024, and the longest of each row is exactly 384.
All inputs are finite; a program needn't handle non-finite values.
Results may differ from a plain program's by a relative error of at most 0.025.
Values may be sent and summed in bfloat16 or wider, within the bound.
A program may use at most 128 MiB of HBM per device.

v0:
```python
import math

import jax
import jax.numpy as jnp
from jax import lax
from jax.sharding import PartitionSpec as P

NOPE = 128
ROPE = 64
VDIM = 128
KV_RANK = 512
DOC_MAX = 384
QB = 128


masked_score = -1e30


def document_index(lengths_row, count):
    ends = jnp.cumsum(lengths_row)
    positions = jnp.arange(count, dtype=jnp.int32)
    return jnp.sum((positions[:, None] >= ends[None, :]).astype(jnp.int32), axis=1)


def attend_backward(queries, keys_padded, values_padded, grads_out, doc_padded, block, window):
    seq_len = queries.shape[0]
    reach = window - block
    scale = 1.0 / math.sqrt(queries.shape[2])
    blocks = seq_len // block

    def one_block(carry, index):
        grad_keys, grad_values = carry
        first = index * block
        query_rows = lax.dynamic_slice_in_dim(queries, first, block, 0)
        key_rows = lax.dynamic_slice_in_dim(keys_padded, first, window, 0)
        value_rows = lax.dynamic_slice_in_dim(values_padded, first, window, 0)
        out_rows = lax.dynamic_slice_in_dim(grads_out, first, block, 0)
        query_doc = lax.dynamic_slice_in_dim(doc_padded, first + reach, block, 0)
        key_doc = lax.dynamic_slice_in_dim(doc_padded, first, window, 0)
        query_pos = jnp.arange(block, dtype=jnp.int32) + reach
        key_pos = jnp.arange(window, dtype=jnp.int32)
        allowed = (key_pos[None, :] <= query_pos[:, None]) & (
            key_doc[None, :] == query_doc[:, None]
        )
        scores = (
            jnp.einsum("qhd,khd->hqk", query_rows, key_rows, preferred_element_type=jnp.float32)
            * scale
        )
        scores = jnp.where(allowed[None], scores, masked_score)
        top = jnp.max(scores, axis=2, keepdims=True)
        weights = jnp.exp(scores - top)
        probs = weights / jnp.sum(weights, axis=2, keepdims=True)
        probs_low = probs.astype(jnp.bfloat16)
        attn_out = jnp.einsum(
            "hqk,khd->qhd", probs_low, value_rows, preferred_element_type=jnp.float32
        )
        delta = jnp.sum(out_rows.astype(jnp.float32) * attn_out, axis=2)
        dprob = jnp.einsum("qhd,khd->hqk", out_rows, value_rows, preferred_element_type=jnp.float32)
        dscore_low = (probs * (dprob - jnp.transpose(delta)[:, :, None])).astype(jnp.bfloat16)
        grad_query = (
            jnp.einsum("hqk,khd->qhd", dscore_low, key_rows, preferred_element_type=jnp.float32)
            * scale
        )
        grad_key_rows = (
            jnp.einsum("hqk,qhd->khd", dscore_low, query_rows, preferred_element_type=jnp.float32)
            * scale
        )
        grad_value_rows = jnp.einsum(
            "hqk,qhd->khd", probs_low, out_rows, preferred_element_type=jnp.float32
        )
        grad_keys = lax.dynamic_update_slice_in_dim(
            grad_keys,
            lax.dynamic_slice_in_dim(grad_keys, first, window, 0) + grad_key_rows,
            first,
            0,
        )
        grad_values = lax.dynamic_update_slice_in_dim(
            grad_values,
            lax.dynamic_slice_in_dim(grad_values, first, window, 0) + grad_value_rows,
            first,
            0,
        )
        return ((grad_keys, grad_values), grad_query.astype(jnp.bfloat16))

    start_keys = jnp.zeros(keys_padded.shape, jnp.float32)
    start_values = jnp.zeros(values_padded.shape, jnp.float32)
    (grad_keys, grad_values), grad_queries = lax.scan(
        one_block, (start_keys, start_values), jnp.arange(blocks, dtype=jnp.int32)
    )
    grad_queries = grad_queries.reshape(seq_len, queries.shape[1] * queries.shape[2])
    return (grad_keys[reach:], grad_values[reach:], grad_queries)


def local(query, latent, d_attn, w_kv, doc_lengths):
    group_size = lax.axis_size("head")
    own_tokens = query.shape[0]
    seq_len = own_tokens * group_size
    head_count = w_kv.shape[1] // (NOPE + VDIM)
    queries, grads_out = (
        lax.all_to_all(query, "head", split_axis=1, concat_axis=0, tiled=True),
        lax.all_to_all(d_attn, "head", split_axis=1, concat_axis=0, tiled=True),
    )
    latents = lax.all_gather(latent, "head", axis=0, tiled=True)
    compressed = latents[:, :KV_RANK]
    whole_weight = lax.all_gather(w_kv, "dp", axis=0, tiled=True)
    kv_up = jnp.dot(compressed, whole_weight, preferred_element_type=jnp.float32)
    kv_up = kv_up.astype(jnp.bfloat16).reshape(seq_len, head_count, NOPE + VDIM)
    rotary = jnp.broadcast_to(latents[:, None, KV_RANK:], (seq_len, head_count, ROPE))
    keys = jnp.concatenate([kv_up[:, :, :NOPE], rotary], axis=2)
    keys_padded = jnp.concatenate(
        [jnp.zeros((DOC_MAX, head_count, NOPE + ROPE), jnp.bfloat16), keys], axis=0
    )
    values_padded = jnp.concatenate(
        [jnp.zeros((DOC_MAX, head_count, VDIM), jnp.bfloat16), kv_up[:, :, NOPE:]], axis=0
    )
    doc_ids = document_index(doc_lengths[0], seq_len)
    doc_padded = jnp.concatenate([jnp.full((DOC_MAX,), -1, jnp.int32), doc_ids])
    grad_keys, grad_values, grad_queries = attend_backward(
        queries.reshape(seq_len, head_count, NOPE + ROPE),
        keys_padded,
        values_padded,
        grads_out.reshape(seq_len, head_count, VDIM),
        doc_padded,
        QB,
        DOC_MAX + QB,
    )
    returned = lax.all_to_all(grad_queries, "head", split_axis=0, concat_axis=1, tiled=True)
    grad_kv = jnp.concatenate([grad_keys[:, :, :NOPE], grad_values], axis=2).astype(jnp.bfloat16)
    grad_kv = grad_kv.reshape(seq_len, head_count * (NOPE + VDIM))
    grad_weight = lax.psum_scatter(
        lax.dot_general(
            compressed, grad_kv, (((0,), (0,)), ((), ())), preferred_element_type=jnp.float32
        ).astype(jnp.bfloat16),
        "dp",
        scatter_dimension=0,
        tiled=True,
    ).astype(jnp.float32)
    grad_compressed = lax.dot_general(
        grad_kv, whole_weight, (((1,), (1,)), ((), ())), preferred_element_type=jnp.float32
    )
    head_terms = jnp.concatenate([grad_compressed, jnp.sum(grad_keys[:, :, NOPE:], axis=1)], axis=1)
    grad_latent = lax.psum_scatter(
        head_terms.astype(jnp.bfloat16), "head", scatter_dimension=0, tiled=True
    ).astype(jnp.float32)
    return (returned, grad_latent, grad_weight)


def solution(mesh):
    placed = (
        P(("dp", "head"), None),
        P(("dp", "head"), None),
        P(("dp", "head"), None),
        P("dp", "head"),
        P("dp", None),
    )
    return jax.shard_map(
        local,
        mesh=mesh,
        in_specs=placed,
        out_specs=(P(("dp", "head"), None), P(("dp", "head"), None), P("dp", "head")),
        check_vma=False,
    )
```

profile of v0, /device:TPU:0, one launch (start us, length us, event | category | flops | bytes accessed | tf_op | source)
XLA Modules:
  0.0 464.4 jit_solution(16384341293036720376)
XLA Ops:
  7.2 3.1 copy.81
  10.3 6.3 %all-to-all-start.1 = ((bf16[128,8,1024]{2,0,1:T(8,128)(2,1)}), bf16[128,8,1024]{2,0,1:T(8,128)(2,1)S(1)}, u32[]{:S(2)}, u32[]{:S(2)}) async-start(bf16[128,8,1024]{2,0,1:T(8,128)(2,1)} %bitcast.77), calls=%async_computation.1 | async-start | bytes 4194304 | tf_op jit(solution)/shard_map/all_to_all | solution.py:101
  17.4 4.6 %copy.52 = bf16[128,12288]{0,1:T(8,128)(2,1)} copy(bf16[128,12288]{1,0:T(8,128)(2,1)} %param.7) | data formatting | bytes 6291456 | tf_op args[0]
  22.0 53.2 %all-to-all-done.1 = bf16[128,8,1024]{2,0,1:T(8,128)(2,1)S(1)} async-done(((bf16[128,8,1024]{2,0,1:T(8,128)(2,1)}), bf16[128,8,1024]{2,0,1:T(8,128)(2,1)S(1)}, u32[]{:S(2)}, u32[]{:S(2)}) %all-to-all-start.1) | async-done | bytes 2097184 | tf_op jit(solution)/shard_map/all_to_all | solution.py:101
  76.5 3.6 all-to-all-start
  81.3 38.3 %all-gather.5.cloned.1.call-done = bf16[512,2048]{1,0:T(8,128)(2,1)} async-done(((bf16[128,2048]{1,0:T(8,128)(2,1)}), bf16[512,2048]{1,0:T(8,128)(2,1)}) %all-gather.5.cloned.1.call-update) | async-done | bytes 2097168 | tf_op jit(solution)/shard_map/all_gather | solution.py:105
  119.6 4.3 convolution_convert_fusion
  128.7 4.2 copy.70
  132.8 3.5 concatenate.23
  136.5 2.3 fusion.58
  140.9 10.7 %all-to-all-done = bf16[128,8,1536]{0,2,1:T(8,128)(2,1)S(1)} async-done(((bf16[128,8,1536]{0,2,1:T(8,128)(2,1)}), bf16[128,8,1536]{0,2,1:T(8,128)(2,1)S(1)}, u32[]{:S(2)}, u32[]{:S(2)}) %all-to-all-start) | async-done | bytes 3145760 | tf_op jit(solution)/shard_map/all_to_all | solution.py:100
  151.6 10.0 %copy.53 = bf16[8,128,1536]{1,0,2:T(8,128)(2,1)} copy(bf16[8,128,1536]{1,2,0:T(8,128)(2,1)S(1)} %bitcast.72) | data formatting | bytes 6291456 | tf_op jit(solution)/shard_map/all_to_all | solution.py:100
  161.7 5.8 %reshape.113 = bf16[1024,8,192]{0,2,1:T(8,128)(2,1)} reshape(bf16[8,128,1536]{1,0,2:T(8,128)(2,1)} %copy.53) | data formatting | bytes 6291456 | tf_op jit(solution)/shard_map/reshape | solution.py:119
  167.5 3.0 broadcast_in_dim.55
  170.5 4.1 broadcast_in_dim.54
  174.6 171.6 %while.16 = (s32[]{:T(128)}, f32[1408,8,192]{0,2,1:T(8,128)}, f32[1408,8,128]{0,2,1:T(8,128)}, bf16[8,128,8,192]{1,3,2,0:T(8,128)(2,1)}, s32[8]{0:T(128)S(1)}, /...) while((s32[]{:T(128)}, f32[1408,8,192]{0,2,1:T(8,128)}, ...), condition=%wide.region_6.7_spmd, body=%wide.region_2.6_spmd.sunk | while | flops 1016004224 | bytes 139232272 | solution.py:87
  177.1 4.0 fusion.105
  181.1 2.6 fusion.106
  185.7 3.5 fusion.109
  192.7 3.3 copy-done
  198.5 4.0 fusion.105
  202.5 2.6 fusion.106
  207.1 3.5 fusion.109
  211.6 2.2 fusion.107
  214.1 3.3 copy-done
  220.0 4.0 fusion.105
  224.0 2.6 fusion.106
  228.6 3.5 fusion.109
  235.6 3.3 copy-done
  241.4 4.0 fusion.105
  245.4 2.6 fusion.106
  250.0 3.5 fusion.109
  254.5 2.3 fusion.107
  257.0 3.3 copy-done
  262.9 4.0 fusion.105
  266.9 2.6 fusion.106
  271.5 3.5 fusion.109
  275.9 2.2 fusion.107
  278.5 3.3 copy-done
  284.3 4.0 fusion.105
  288.3 2.6 fusion.106
  292.9 3.5 fusion.109
  297.4 2.2 fusion.107
  299.9 3.3 copy-done
  305.8 4.0 fusion.105
  309.8 2.6 fusion.106
  314.4 3.5 fusion.109
  321.4 3.3 copy-done
  327.2 4.0 fusion.105
  331.2 2.6 fusion.106
  335.8 3.5 fusion.109
  340.3 2.3 fusion.107
  342.8 3.3 copy-done
  347.9 2.5 slice.47
  350.5 2.5 slice.46
  355.0 2.3 convolution_convert_fusion.2
  358.9 4.7 %copy.58 = bf16[8,128,1536]{2,1,0:T(8,128)(2,1)} copy(bf16[8,128,1536]{1,2,0:T(8,128)(2,1)} %bitcast.82) | data formatting | bytes 6291456 | tf_op jit(solution)/shard_map/all_to_all | solution.py:127
  363.6 3.6 all-to-all-start.2
  367.3 6.2 %fusion.59 = bf16[512,2048]{0,1:T(8,128)(2,1)} fusion(bf16[1024,2048]{0,1:T(8,128)(2,1)} %bitcast.80, bf16[1024,576]{0,1:T(8,128)(2,1)} %all-gather.3.cloned.1.call-done), kind=kOutput, calls=%fused_computation.52 | convolution fusion | flops 2148532224 | bytes 7340032 | tf_op jit(solution)/shard_map/dot_general | solution.py:131
  373.5 4.0 copy.67
  377.5 22.6 %reduce-scatter.7.cloned.1.call-done = bf16[128,576]{1,0:T(8,128)(2,1)} async-done(((bf16[1024,576]{1,0:T(8,128)(2,1)}), bf16[128,576]{1,0:T(8,128)(2,1)}) %reduce-scatter.7.cloned.1.call-update) | async-done | bytes 147472
  401.9 44.4 %reduce-scatter.9.cloned.1.call-done = bf16[128,2048]{1,0:T(8,128)(2,1)} async-done(((bf16[512,2048]{1,0:T(8,128)(2,1)}), bf16[128,2048]{1,0:T(8,128)(2,1)}) %reduce-scatter.9.cloned.1.call-update) | async-done | bytes 524304
  450.5 2.8 copy.59
  453.3 4.6 copy.60
  (245 shorter events, 68.6 us)
Async XLA Ops:
  10.3 64.9 %all-to-all-start.1 = ((bf16[128,8,1024]{2,0,1:T(8,128)(2,1)}), bf16[128,8,1024]{2,0,1:T(8,128)(2,1)S(1)}, u32[]{:S(2)}, u32[]{:S(2)}) async-start(bf16[128,8,1024]{2,0,1:T(8,128)(2,1)} %bitcast.77), calls=%async_computation.1 | async-start | bytes 4194304 | tf_op jit(solution)/shard_map/all_to_all | solution.py:101
  16.6 64.6 %all-gather.3.cloned.1.call-start = ((), (), s32[]{:S(2)}) async-start(), calls=%async_computation.5 | async-start | bytes 1327104 | tf_op jit(solution)/shard_map/all_gather | solution.py:103
  75.2 5.8 %copy-start.7 = (s32[1,5]{1,0:T(1,128)S(1)}, s32[1,5]{1,0:T(1,128)}, u32[]{:S(2)}) copy-start(s32[1,5]{1,0:T(1,128)} %param.11) | copy-start | bytes 64
  76.5 75.1 %all-to-all-start = ((bf16[128,8,1536]{0,2,1:T(8,128)(2,1)}), bf16[128,8,1536]{0,2,1:T(8,128)(2,1)S(1)}, u32[]{:S(2)}, u32[]{:S(2)}) async-start(bf16[128,8,1536]{0,2,1:T(8,128)(2,1)} %bitcast.7), calls=%async_computation | async-start | bytes 6291456 | tf_op jit(solution)/shard_map/all_to_all | solution.py:100
  80.2 39.4 %all-gather.5.cloned.1.call-start = ((), (), s32[]{:S(2)}) async-start(), calls=%async_computation.6 | async-start | bytes 2621440 | tf_op jit(solution)/shard_map/all_gather | solution.py:105
  80.9 319.1 %reduce-scatter.7.cloned.1.call-start = ((), (), s32[]{:S(2)}) async-start(), calls=%async_computation.7 | async-start | bytes 1474560
  132.8 3.5 slice-start.5
  132.8 3.7 copy-start.2
  177.1 12.1 %slice-start.3 = ((s8[5767168]{0:T(1024)(128)(4,1)}), s8[1572864]{0:T(1024)(128)(4,1)S(1)}, s32[]{:S(2)}) async-start(s8[5767168]{0:T(1024)(128)(4,1)} %bitcast.74), calls=%async_computation.12 | async-start | bytes 3145728 | tf_op jit(solution)/shard_map/while
  181.1 2.6 copy-start.8
  181.1 8.1 %slice-start.4 = ((s8[5767168]{0:T(1024)(128)(4,1)}), s8[4194304]{0:T(1024)(128)(4,1)S(1)}, s32[]{:S(2)}) async-start(s8[5767168]{0:T(1024)(128)(4,1)} %bitcast.74), calls=%async_computation.13 | async-start | bytes 8388608 | tf_op jit(solution)/shard_map/while
  183.7 6.2 %slice-start = ((s8[8650752]{0:T(1024)(128)(4,1)}), s8[4194304]{0:T(1024)(128)(4,1)S(1)}, s32[]{:S(2)}) async-start(s8[8650752]{0:T(1024)(128)(4,1)} %bitcast.69), calls=%async_computation.9 | async-start | bytes 8388608 | tf_op jit(solution)/shard_map/while
  183.7 6.2 %slice-start.1 = ((s8[8650752]{0:T(1024)(128)(4,1)}), s8[4194304]{0:T(1024)(128)(4,1)S(1)}, s32[]{:S(2)}) async-start(s8[8650752]{0:T(1024)(128)(4,1)} %bitcast.69), calls=%async_computation.10 | async-start | bytes 8388608 | tf_op jit(solution)/shard_map/while
  190.1 2.5 copy-start.1
  192.7 3.4 copy-start
  198.5 12.1 %slice-start.3 = ((s8[5767168]{0:T(1024)(128)(4,1)}), s8[1572864]{0:T(1024)(128)(4,1)S(1)}, s32[]{:S(2)}) async-start(s8[5767168]{0:T(1024)(128)(4,1)} %bitcast.74), calls=%async_computation.12 | async-start | bytes 3145728 | tf_op jit(solution)/shard_map/while
  202.5 2.6 copy-start.8
  202.5 8.1 %slice-start.4 = ((s8[5767168]{0:T(1024)(128)(4,1)}), s8[4194304]{0:T(1024)(128)(4,1)S(1)}, s32[]{:S(2)}) async-start(s8[5767168]{0:T(1024)(128)(4,1)} %bitcast.74), calls=%async_computation.13 | async-start | bytes 8388608 | tf_op jit(solution)/shard_map/while
  205.1 6.2 %slice-start = ((s8[8650752]{0:T(1024)(128)(4,1)}), s8[4194304]{0:T(1024)(128)(4,1)S(1)}, s32[]{:S(2)}) async-start(s8[8650752]{0:T(1024)(128)(4,1)} %bitcast.69), calls=%async_computation.9 | async-start | bytes 8388608 | tf_op jit(solution)/shard_map/while
  205.1 6.2 %slice-start.1 = ((s8[8650752]{0:T(1024)(128)(4,1)}), s8[4194304]{0:T(1024)(128)(4,1)S(1)}, s32[]{:S(2)}) async-start(s8[8650752]{0:T(1024)(128)(4,1)} %bitcast.69), calls=%async_computation.10 | async-start | bytes 8388608 | tf_op jit(solution)/shard_map/while
  211.6 2.5 copy-start.1
  214.1 3.4 copy-start
  220.0 12.1 %slice-start.3 = ((s8[5767168]{0:T(1024)(128)(4,1)}), s8[1572864]{0:T(1024)(128)(4,1)S(1)}, s32[]{:S(2)}) async-start(s8[5767168]{0:T(1024)(128)(4,1)} %bitcast.74), calls=%async_computation.12 | async-start | bytes 3145728 | tf_op jit(solution)/shard_map/while
  224.0 2.6 copy-start.8
  224.0 8.1 %slice-start.4 = ((s8[5767168]{0:T(1024)(128)(4,1)}), s8[4194304]{0:T(1024)(128)(4,1)S(1)}, s32[]{:S(2)}) async-start(s8[5767168]{0:T(1024)(128)(4,1)} %bitcast.74), calls=%async_computation.13 | async-start | bytes 8388608 | tf_op jit(solution)/shard_map/while
  226.6 6.2 %slice-start = ((s8[8650752]{0:T(1024)(128)(4,1)}), s8[4194304]{0:T(1024)(128)(4,1)S(1)}, s32[]{:S(2)}) async-start(s8[8650752]{0:T(1024)(128)(4,1)} %bitcast.69), calls=%async_computation.9 | async-start | bytes 8388608 | tf_op jit(solution)/shard_map/while
  226.6 6.2 %slice-start.1 = ((s8[8650752]{0:T(1024)(128)(4,1)}), s8[4194304]{0:T(1024)(128)(4,1)S(1)}, s32[]{:S(2)}) async-start(s8[8650752]{0:T(1024)(128)(4,1)} %bitcast.69), calls=%async_computation.10 | async-start | bytes 8388608 | tf_op jit(solution)/shard_map/while
  235.6 3.4 copy-start
  241.4 12.1 %slice-start.3 = ((s8[5767168]{0:T(1024)(128)(4,1)}), s8[1572864]{0:T(1024)(128)(4,1)S(1)}, s32[]{:S(2)}) async-start(s8[5767168]{0:T(1024)(128)(4,1)} %bitcast.74), calls=%async_computation.12 | async-start | bytes 3145728 | tf_op jit(solution)/shard_map/while
  245.4 2.6 copy-start.8
  245.4 8.1 %slice-start.4 = ((s8[5767168]{0:T(1024)(128)(4,1)}), s8[4194304]{0:T(1024)(128)(4,1)S(1)}, s32[]{:S(2)}) async-start(s8[5767168]{0:T(1024)(128)(4,1)} %bitcast.74), calls=%async_computation.13 | async-start | bytes 8388608 | tf_op jit(solution)/shard_map/while
  248.0 6.2 %slice-start = ((s8[8650752]{0:T(1024)(128)(4,1)}), s8[4194304]{0:T(1024)(128)(4,1)S(1)}, s32[]{:S(2)}) async-start(s8[8650752]{0:T(1024)(128)(4,1)} %bitcast.69), calls=%async_computation.9 | async-start | bytes 8388608 | tf_op jit(solution)/shard_map/while
  248.0 6.2 %slice-start.1 = ((s8[8650752]{0:T(1024)(128)(4,1)}), s8[4194304]{0:T(1024)(128)(4,1)S(1)}, s32[]{:S(2)}) async-start(s8[8650752]{0:T(1024)(128)(4,1)} %bitcast.69), calls=%async_computation.10 | async-start | bytes 8388608 | tf_op jit(solution)/shard_map/while
  254.5 2.5 copy-start.1
  257.0 3.4 copy-start
  262.9 12.1 %slice-start.3 = ((s8[5767168]{0:T(1024)(128)(4,1)}), s8[1572864]{0:T(1024)(128)(4,1)S(1)}, s32[]{:S(2)}) async-start(s8[5767168]{0:T(1024)(128)(4,1)} %bitcast.74), calls=%async_computation.12 | async-start | bytes 3145728 | tf_op jit(solution)/shard_map/while
  266.9 2.6 copy-start.8
  266.9 8.1 %slice-start.4 = ((s8[5767168]{0:T(1024)(128)(4,1)}), s8[4194304]{0:T(1024)(128)(4,1)S(1)}, s32[]{:S(2)}) async-start(s8[5767168]{0:T(1024)(128)(4,1)} %bitcast.74), calls=%async_computation.13 | async-start | bytes 8388608 | tf_op jit(solution)/shard_map/while
  269.5 6.2 %slice-start = ((s8[8650752]{0:T(1024)(128)(4,1)}), s8[4194304]{0:T(1024)(128)(4,1)S(1)}, s32[]{:S(2)}) async-start(s8[8650752]{0:T(1024)(128)(4,1)} %bitcast.69), calls=%async_computation.9 | async-start | bytes 8388608 | tf_op jit(solution)/shard_map/while
  269.5 6.2 %slice-start.1 = ((s8[8650752]{0:T(1024)(128)(4,1)}), s8[4194304]{0:T(1024)(128)(4,1)S(1)}, s32[]{:S(2)}) async-start(s8[8650752]{0:T(1024)(128)(4,1)} %bitcast.69), calls=%async_computation.10 | async-start | bytes 8388608 | tf_op jit(solution)/shard_map/while
  275.9 2.5 copy-start.1
  278.5 3.4 copy-start
  284.3 12.1 %slice-start.3 = ((s8[5767168]{0:T(1024)(128)(4,1)}), s8[1572864]{0:T(1024)(128)(4,1)S(1)}, s32[]{:S(2)}) async-start(s8[5767168]{0:T(1024)(128)(4,1)} %bitcast.74), calls=%async_computation.12 | async-start | bytes 3145728 | tf_op jit(solution)/shard_map/while
  288.3 2.6 copy-start.8
  288.3 8.1 %slice-start.4 = ((s8[5767168]{0:T(1024)(128)(4,1)}), s8[4194304]{0:T(1024)(128)(4,1)S(1)}, s32[]{:S(2)}) async-start(s8[5767168]{0:T(1024)(128)(4,1)} %bitcast.74), calls=%async_computation.13 | async-start | bytes 8388608 | tf_op jit(solution)/shard_map/while
  290.9 6.2 %slice-start = ((s8[8650752]{0:T(1024)(128)(4,1)}), s8[4194304]{0:T(1024)(128)(4,1)S(1)}, s32[]{:S(2)}) async-start(s8[8650752]{0:T(1024)(128)(4,1)} %bitcast.69), calls=%async_computation.9 | async-start | bytes 8388608 | tf_op jit(solution)/shard_map/while
  290.9 6.2 %slice-start.1 = ((s8[8650752]{0:T(1024)(128)(4,1)}), s8[4194304]{0:T(1024)(128)(4,1)S(1)}, s32[]{:S(2)}) async-start(s8[8650752]{0:T(1024)(128)(4,1)} %bitcast.69), calls=%async_computation.10 | async-start | bytes 8388608 | tf_op jit(solution)/shard_map/while
  297.4 2.5 copy-start.1
  299.9 3.4 copy-start
  305.8 12.1 %slice-start.3 = ((s8[5767168]{0:T(1024)(128)(4,1)}), s8[1572864]{0:T(1024)(128)(4,1)S(1)}, s32[]{:S(2)}) async-start(s8[5767168]{0:T(1024)(128)(4,1)} %bitcast.74), calls=%async_computation.12 | async-start | bytes 3145728 | tf_op jit(solution)/shard_map/while
  309.8 2.6 copy-start.8
  309.8 8.1 %slice-start.4 = ((s8[5767168]{0:T(1024)(128)(4,1)}), s8[4194304]{0:T(1024)(128)(4,1)S(1)}, s32[]{:S(2)}) async-start(s8[5767168]{0:T(1024)(128)(4,1)} %bitcast.74), calls=%async_computation.13 | async-start | bytes 8388608 | tf_op jit(solution)/shard_map/while
  312.4 6.2 %slice-start = ((s8[8650752]{0:T(1024)(128)(4,1)}), s8[4194304]{0:T(1024)(128)(4,1)S(1)}, s32[]{:S(2)}) async-start(s8[8650752]{0:T(1024)(128)(4,1)} %bitcast.69), calls=%async_computation.9 | async-start | bytes 8388608 | tf_op jit(solution)/shard_map/while
  312.4 6.2 %slice-start.1 = ((s8[8650752]{0:T(1024)(128)(4,1)}), s8[4194304]{0:T(1024)(128)(4,1)S(1)}, s32[]{:S(2)}) async-start(s8[8650752]{0:T(1024)(128)(4,1)} %bitcast.69), calls=%async_computation.10 | async-start | bytes 8388608 | tf_op jit(solution)/shard_map/while
  321.4 3.4 copy-start
  327.2 12.1 %slice-start.3 = ((s8[5767168]{0:T(1024)(128)(4,1)}), s8[1572864]{0:T(1024)(128)(4,1)S(1)}, s32[]{:S(2)}) async-start(s8[5767168]{0:T(1024)(128)(4,1)} %bitcast.74), calls=%async_computation.12 | async-start | bytes 3145728 | tf_op jit(solution)/shard_map/while
  331.2 2.6 copy-start.8
  331.2 8.1 %slice-start.4 = ((s8[5767168]{0:T(1024)(128)(4,1)}), s8[4194304]{0:T(1024)(128)(4,1)S(1)}, s32[]{:S(2)}) async-start(s8[5767168]{0:T(1024)(128)(4,1)} %bitcast.74), calls=%async_computation.13 | async-start | bytes 8388608 | tf_op jit(solution)/shard_map/while
  333.8 6.2 %slice-start = ((s8[8650752]{0:T(1024)(128)(4,1)}), s8[4194304]{0:T(1024)(128)(4,1)S(1)}, s32[]{:S(2)}) async-start(s8[8650752]{0:T(1024)(128)(4,1)} %bitcast.69), calls=%async_computation.9 | async-start | bytes 8388608 | tf_op jit(solution)/shard_map/while
  333.8 6.2 %slice-start.1 = ((s8[8650752]{0:T(1024)(128)(4,1)}), s8[4194304]{0:T(1024)(128)(4,1)S(1)}, s32[]{:S(2)}) async-start(s8[8650752]{0:T(1024)(128)(4,1)} %bitcast.69), calls=%async_computation.10 | async-start | bytes 8388608 | tf_op jit(solution)/shard_map/while
  342.8 3.4 copy-start
  353.5 3.8 copy-start.5
  363.6 86.9 %all-to-all-start.2 = ((bf16[8,128,1536]{2,1,0:T(8,128)(2,1)}), bf16[8,128,1536]{2,1,0:T(8,128)(2,1)S(1)}, u32[]{:S(2)}, u32[]{:S(2)}) async-start(bf16[8,128,1536]{2,1,0:T(8,128)(2,1)} %copy.58), calls=%async_computation.2 | async-start | bytes 6291456 | tf_op jit(solution)/shard_map/all_to_all | solution.py:127
  367.3 79.0 %reduce-scatter.9.cloned.1.call-start = ((), (), s32[]{:S(2)}) async-start(), calls=%async_computation.8 | async-start | bytes 2621440
  (14 other events, 21.0 us)
Sparse Core Ops, SparseCore 0:
  19.1 49.0 all-gather.2
  82.9 36.6 all-gather.4
  359.1 40.9 reduce-scatter.6
  402.9 43.2 reduce-scatter.8
where the time goes:
time: 466 us; the launch traced here: 464 us
  waiting for transfers between devices  171 us (37%)
  matrix products  133 us (29%)
  local copies, waits for them, and re-layouts  121 us (26%)
  between operations  13.9 us (3%)
  starting transfers between devices  13.8 us (3%)
  other arithmetic  6.66 us (1%)
  loops' own time  6.01 us (1%)
    unnamed x6, waiting for transfers between devices  68.3 us
    all_to_all x1, waiting for transfers between devices, local(): lax.all_to_all(d_attn, 'head', split_axis=1, concat_axis=0, tiled=True)  53.2 us
    all_gather x1, waiting for transfers between devices, local(): whole_weight = lax.all_gather(w_kv, 'dp', axis=0, tiled=True)  38.3 us
    unnamed x23, local copies, waits for them, and re-layouts  32.3 us
    sub x8, matrix products, one_block(): weights = jnp.exp(scores - top)  32 us
    while x128, local copies, waits for them, and re-layouts  31 us
    dot_general x8, matrix products, one_block(): jnp.einsum('hqk,khd->qhd', dscore_low, key_rows, preferred_element_type=j...  27.8 us
    dot_general x8, matrix products, one_block(): jnp.einsum('hqk,khd->qhd', probs_low, value_rows, preferred_element_type=...  20.7 us
  transfers between devices with their start and end apart: 7, of which 5 were waited for; matrix products, arithmetic and copies ran while one was open for 10% of the time, Pallas kernels for 0%

commit v1 on v0

v1 whole, which is shorter than its diff:
```python
import functools
import math

import jax
import jax.numpy as jnp
from jax import lax
from jax.experimental import pallas as pl
from jax.experimental.pallas import tpu as pltpu
from jax.sharding import PartitionSpec as P

NOPE = 128
ROPE = 64
VDIM = 128
KV_RANK = 512
DOC_MAX = 384
QB = 128
MEMBERS = 4
MESH = pl.DeviceIdType.MESH

masked_score = -1e30
NN = (((1,), (0,)), ((), ()))
NT = (((1,), (1,)), ((), ()))
TN = (((0,), (0,)), ((), ()))


def dot(a, b, dims):
    return lax.dot_general(a, b, dims, preferred_element_type=jnp.float32)


def kernel(
    cfg,
    query,
    d_attn,
    latent,
    latent_t,
    w,
    starts,
    d_query,
    d_w,
    d_lat,
    q_buf,
    o_buf,
    dq_buf,
    keys,
    vals,
    dk_acc,
    dv_acc,
    dkv,
    dlat_acc,
    rope_acc,
    q_send,
    q_recv,
    o_send,
    o_recv,
    dq_send,
    dq_recv,
):
    members, parts, pairs, own = cfg
    chunks = parts * pairs
    dp = lax.axis_index("dp")
    head = lax.axis_index("head")
    part = head // members
    me = lax.rem(head, members)
    window = latent.shape[0]
    reach = window - members * own
    qw = 2 * (NOPE + ROPE)
    ow = 2 * VDIM
    scale = 1.0 / math.sqrt(NOPE + ROPE)
    to_exp2 = scale * math.log2(math.e)

    def other(k):
        return lax.rem(me + k, members)

    def place(c):
        return lax.rem(part + c // pairs, parts), lax.rem(c, pairs)

    def pair_index(member, c):
        p, j = place(c)
        return (member + members * p) * pairs + j

    barrier = pltpu.get_barrier_semaphore()
    for k in range(1, members):
        pl.semaphore_signal(
            barrier, inc=1, device_id=(dp, part * members + other(k)), device_id_type=MESH
        )
    pl.semaphore_wait(barrier, members - 1)

    def move(src, dst, send, recv, c, k):
        if k == 0:
            return pltpu.make_async_copy(src, dst, send.at[c, 0])
        return pltpu.make_async_remote_copy(
            src_ref=src,
            dst_ref=dst,
            send_sem=send.at[c, k],
            recv_sem=recv.at[c, k],
            device_id=(dp, part * members + other(k)),
            device_id_type=MESH,
        )

    def q_copy(c, k):
        col = pl.multiple_of(pair_index(other(k), c) * qw, 128)
        row = pl.multiple_of(me * own, own)
        return move(
            query.at[:, pl.ds(col, qw)], q_buf.at[c, pl.ds(row, own)], q_send, q_recv, c, k
        )

    def o_copy(c, k):
        col = pl.multiple_of(pair_index(other(k), c) * ow, 128)
        row = pl.multiple_of(me * own, own)
        return move(
            d_attn.at[:, pl.ds(col, ow)], o_buf.at[c, pl.ds(row, own)], o_send, o_recv, c, k
        )

    def dq_copy(c, k):
        col = pl.multiple_of(pair_index(me, c) * qw, 128)
        row = pl.multiple_of(other(k) * own, own)
        return move(
            dq_buf.at[c, pl.ds(row, own)], d_query.at[:, pl.ds(col, qw)], dq_send, dq_recv, c, k
        )

    @pl.loop(0, chunks)
    def _(c):
        for k in list(range(1, members)) + [0]:
            q_copy(c, k).start()
            o_copy(c, k).start()

    dlat_acc[...] = jnp.zeros_like(dlat_acc)
    rope_acc[...] = jnp.zeros_like(rope_acc)
    rope = latent[:, KV_RANK:].astype(jnp.float32)
    empty = jnp.zeros_like(rope)
    half = NOPE // 2
    keys[0, :, NOPE:] = jnp.concatenate([rope, empty], axis=1).astype(jnp.bfloat16)
    keys[2] = jnp.concatenate([empty, rope, empty, rope], axis=1).astype(jnp.bfloat16)
    lane = lax.broadcasted_iota(jnp.int32, (window, NOPE), 1)

    @pl.loop(0, chunks)
    def _(c):
        p, j = place(c)
        cols = pl.ds(pl.multiple_of(j * 512, 512), 2 * (NOPE + VDIM))
        kv = dot(latent[:, :KV_RANK], w[p, :, cols], NN)
        keys[0, :, :NOPE] = kv[:, :NOPE].astype(jnp.bfloat16)
        vals[0] = kv[:, NOPE : 2 * NOPE].astype(jnp.bfloat16)
        rolled = pltpu.roll(kv[:, 2 * NOPE : 3 * NOPE], half, 1)
        keys[1, :, :NOPE] = jnp.where(lane < half, 0.0, rolled).astype(jnp.bfloat16)
        keys[1, :, NOPE:] = jnp.where(
            lane < half, rolled.astype(jnp.bfloat16).astype(jnp.float32),
            keys[2, :, NOPE:].astype(jnp.float32),
        ).astype(jnp.bfloat16)
        vals[1] = kv[:, 3 * NOPE :].astype(jnp.bfloat16)
        for k in range(members):
            if k == 0:
                q_copy(c, k).wait()
                o_copy(c, k).wait()
            else:
                q_copy(c, k).wait_recv()
                o_copy(c, k).wait_recv()
        dk_acc[...] = jnp.zeros_like(dk_acc)
        dv_acc[...] = jnp.zeros_like(dv_acc)
        for b in range(members * own // QB):
            rows = slice(b * QB, (b + 1) * QB)
            span = slice(b * QB, b * QB + reach + QB)
            shape = (reach + QB, QB)
            key_pos = lax.broadcasted_iota(jnp.int32, shape, 0) + b * QB
            query_pos = lax.broadcasted_iota(jnp.int32, shape, 1) + (reach + b * QB)
            allowed = (key_pos <= query_pos) & (key_pos >= starts[:, rows])
            grads = []
            for h in range(2):
                q = q_buf[c, rows, h * NOPE : h * NOPE + 2 * NOPE]
                o = o_buf[c, rows, h * VDIM : (h + 1) * VDIM]
                key = keys[h, span]
                s = dot(key, q, NT)
                s = jnp.where(allowed, s, masked_score)
                top = jnp.max(s, axis=0, keepdims=True)
                e = jnp.exp2((s - top) * to_exp2)
                probs = e * (1.0 / jnp.sum(e, axis=0, keepdims=True))
                low = probs.astype(jnp.bfloat16)
                dprob = dot(vals[h, span], o, NT)
                delta = jnp.sum(low.astype(jnp.float32) * dprob, axis=0, keepdims=True)
                ds = (probs * (dprob - delta)).astype(jnp.bfloat16)
                dv_acc[h, span] += dot(low, o, NN)
                dk_acc[h, span] += dot(ds, q, NN)
                grads.append(dot(ds, key, TN) * scale)
            a, z = grads
            dq_buf[c, rows, :NOPE] = a[:, :NOPE].astype(jnp.bfloat16)
            dq_buf[c, rows, NOPE : 2 * NOPE] = (a[:, NOPE:] + z[:, :NOPE]).astype(jnp.bfloat16)
            dq_buf[c, rows, 2 * NOPE :] = z[:, NOPE:].astype(jnp.bfloat16)
        for k in list(range(1, members)) + [0]:
            dq_copy(c, k).start()
        low_lane = lane < half
        dkv[:, :NOPE] = (dk_acc[0, :, :NOPE] * scale).astype(jnp.bfloat16)
        dkv[:, NOPE : 2 * NOPE] = dv_acc[0].astype(jnp.bfloat16)
        turned_a = pltpu.roll(dk_acc[1, :, :NOPE], half, 1)
        turned_b = pltpu.roll(dk_acc[1, :, NOPE:], half, 1)
        dkv[:, 2 * NOPE : 3 * NOPE] = (
            jnp.where(low_lane, turned_a, turned_b) * scale
        ).astype(jnp.bfloat16)
        dkv[:, 3 * NOPE :] = dv_acc[1].astype(jnp.bfloat16)
        rope_acc[...] += dk_acc[0, :, NOPE:] + turned_b
        dlat_acc[...] += dot(dkv[...], w[p, :, cols], NT)
        d_w[p, :, cols] = dot(latent_t[...], dkv[...], NN).astype(jnp.bfloat16)

    d_lat[:, :KV_RANK] = dlat_acc[...]
    d_lat[:, KV_RANK:] = rope_acc[:, :ROPE] * scale

    @pl.loop(0, chunks)
    def _(c):
        for k in range(members):
            if k == 0:
                dq_copy(c, k).wait()
            else:
                q_copy(c, k).wait_send()
                o_copy(c, k).wait_send()
                dq_copy(c, k).wait()


def local(query, latent, d_attn, w_kv, doc_lengths):
    group = lax.axis_size("head")
    head = lax.axis_index("head")
    own = query.shape[0]
    members = min(MEMBERS, group)
    parts = group // members
    seq = own * group
    held = members * own
    pairs = w_kv.shape[1] // (2 * (NOPE + VDIM))
    chunks = parts * pairs
    window = DOC_MAX + held
    first = (head // members) * held
    across = [[m + members * p for p in range(parts)] for m in range(members)]

    latents = lax.all_gather(latent, "head", axis=0, tiled=True)
    padded = jnp.concatenate([jnp.zeros((DOC_MAX, latent.shape[1]), latent.dtype), latents], axis=0)
    near = lax.dynamic_slice_in_dim(padded, first, window, 0)
    both = lax.all_gather(w_kv, "head", axis=0, axis_index_groups=across)
    weight = lax.all_gather(both, "dp", axis=1, tiled=True)

    ends = jnp.cumsum(doc_lengths[0])
    positions = first + jnp.arange(held, dtype=jnp.int32)
    starts = jnp.max(jnp.where(ends[None, :] <= positions[:, None], ends[None, :], 0), axis=1)
    starts = (starts - first + DOC_MAX).astype(jnp.int32)[None, :]

    hbm = pl.BlockSpec(memory_space=pl.ANY)
    vmem = pl.BlockSpec(memory_space=pltpu.VMEM)
    bf16, f32 = jnp.bfloat16, jnp.float32
    qw, ow, cw = 2 * (NOPE + ROPE), 2 * VDIM, 2 * (NOPE + VDIM)
    sems = [pltpu.SemaphoreType.DMA((chunks, members))] * 6
    d_query, d_w, d_lat = pl.pallas_call(
        functools.partial(kernel, (members, parts, pairs, own)),
        out_shape=(
            jax.ShapeDtypeStruct(query.shape, bf16),
            jax.ShapeDtypeStruct(weight.shape, bf16),
            jax.ShapeDtypeStruct(near.shape, f32),
        ),
        in_specs=[hbm, hbm, vmem, vmem, vmem, vmem],
        out_specs=(hbm, vmem, vmem),
        scratch_shapes=[
            pltpu.VMEM((chunks, held, qw), bf16),
            pltpu.VMEM((chunks, held, ow), bf16),
            pltpu.VMEM((chunks, held, qw), bf16),
            pltpu.VMEM((3, window, 2 * NOPE), bf16),
            pltpu.VMEM((2, window, VDIM), bf16),
            pltpu.VMEM((2, window, 2 * NOPE), f32),
            pltpu.VMEM((2, window, VDIM), f32),
            pltpu.VMEM((window, cw), bf16),
            pltpu.VMEM((window, KV_RANK), f32),
            pltpu.VMEM((window, NOPE), f32),
        ]
        + sems,
        compiler_params=pltpu.CompilerParams(
            collective_id=0, has_side_effects=True, vmem_limit_bytes=56 * 2**20
        ),
    )(query, d_attn, near, jnp.transpose(near[:, :KV_RANK]), weight, starts)

    grad_w = lax.psum_scatter(d_w, "dp", scatter_dimension=1, tiled=True)
    grad_w = lax.psum_scatter(grad_w, "head", scatter_dimension=0, axis_index_groups=across)
    whole = lax.dynamic_update_slice_in_dim(
        jnp.zeros((DOC_MAX + seq, near.shape[1]), bf16), d_lat.astype(bf16), first, 0
    )
    grad_latent = lax.psum_scatter(whole[DOC_MAX:], "head", scatter_dimension=0, tiled=True)
    return (d_query, grad_latent.astype(f32), grad_w.astype(f32))


def solution(mesh):
    placed = (
        P(("dp", "head"), None),
        P(("dp", "head"), None),
        P(("dp", "head"), None),
        P("dp", "head"),
        P("dp", None),
    )
    return jax.shard_map(
        local,
        mesh=mesh,
        in_specs=placed,
        out_specs=(P(("dp", "head"), None), P(("dp", "head"), None), P("dp", "head")),
        check_vma=False,
    )
```

time: 466 us -> 357 us (0.77)
  matrix products: 133 us -> 0 us
  local copies, waits for them, and re-layouts: 121 us -> 11 us
  Pallas kernels: 0 us -> 99.5 us
  waiting for transfers between devices: 171 us -> 228 us
  starting transfers between devices: 13.8 us -> 0.23 us
  loops' own time: 6.01 us -> 0 us
    dot_general x43 -> x0, matrix products: 101 us -> none  [the longest x8 27.8 us: one_block(): jnp.einsum('hqk,khd->qhd', dscore_low, key_rows, preferred_element_type=j...]
    pallas_call x0 -> x1, Pallas kernels: none -> 99.5 us  [local(): pl.pallas_call(functools.partial(kernel, (members, parts, pairs, own)), o...]
    reduce_scatter x0 -> x2, waiting for transfers between devices: none -> 79.6 us  [the longest x1 48.6 us: local(): grad_w = lax.psum_scatter(d_w, 'dp', scatter_dimension=1, tiled=True)]
    all_to_all x3 -> x0, waiting for transfers between devices: 63.9 us -> none  [the longest x1 53.2 us: local(): lax.all_to_all(d_attn, 'head', split_axis=1, concat_axis=0, tiled=True)]
    all_gather x1 -> x2, waiting for transfers between devices: 38.3 us -> 86.7 us  [the longest x1 49.6 us: local(): weight = lax.all_gather(both, 'dp', axis=1, tiled=True)]
    sub x8 -> x0, matrix products: 32 us -> none  [one_block(): weights = jnp.exp(scores - top)]
    while x128 -> x0, local copies, waits for them, and re-layouts: 31 us -> none
    unnamed x6 -> x7, waiting for transfers between devices: 68.3 us -> 37.6 us
  transfers between devices with their start and end apart: 7 -> 6, of which waited for: 5 -> 6; matrix products, arithmetic and copies ran while one was open for 10% -> 3% of each run, Pallas kernels for 0% -> 0%
where the time goes in v1:
time: 357 us
  waiting for transfers between devices  228 us (64%)
  Pallas kernels  99.5 us (28%)
  between operations  14.2 us (4%)
  local copies, waits for them, and re-layouts  11 us (3%)
  other arithmetic  3.84 us (1%)
    pallas_call x1, Pallas kernels, local(): pl.pallas_call(functools.partial(kernel, (members, parts, pairs, own)), o...  99.5 us
    all_gather x1, waiting for transfers between devices, local(): weight = lax.all_gather(both, 'dp', axis=1, tiled=True)  49.6 us
    reduce_scatter x1, waiting for transfers between devices, local(): grad_w = lax.psum_scatter(d_w, 'dp', scatter_dimension=1, tiled=True)  48.6 us
    unnamed x7, waiting for transfers between devices  37.6 us
    all_gather x1, waiting for transfers between devices, local(): both = lax.all_gather(w_kv, 'head', axis=0, axis_index_groups=across)  37.1 us
    reduce_scatter x1, waiting for transfers between devices, local(): lax.psum_scatter(grad_w, 'head', scatter_dimension=0, axis_index_groups=a...  31 us
    all_gather x1, waiting for transfers between devices, local(): latents = lax.all_gather(latent, 'head', axis=0, tiled=True)  24.4 us
  transfers between devices with their start and end apart: 6, of which 6 were waited for; matrix products, arithmetic and copies ran while one was open for 3% of the time, Pallas kernels for 0%

profile of v1, /device:TPU:0, one launch (start us, length us, event | category | flops | bytes accessed | tf_op | source)
XLA Modules:
  0.0 357.1 jit_solution(12608295969130979077)
XLA Ops:
  7.2 0.0 copy-start.3
  7.2 0.0 all-gather.9.cloned.1.call-start
  7.2 0.7 all-gather.9.cloned.1.call-update
  7.9 0.0 all-gather.5.cloned.1.call-start
  8.0 0.7 all-gather.5.cloned.1.call-update
  8.7 0.0 all-gather.7.cloned.1.call-start
  8.7 37.1 %all-gather.9.cloned.1.call-done = bf16[256,2048]{1,0:T(8,128)(2,1)} async-done(((bf16[128,2048]{1,0:T(8,128)(2,1)}), bf16[256,2048]{1,0:T(8,128)(2,1)}) %all-gather.9.cloned.1.call-update) | async-done | bytes 1048592 | tf_op jit(solution)/shard_map/all_gather | solution.py:233
  45.8 0.0 all-gather.7.cloned.1.call-update
  45.8 0.0 reduce-scatter.6.cloned.1.call-start
  45.9 0.0 copy-done.3
  45.9 0.2 reduce-window.8
  46.0 0.1 select_reduce_fusion
  46.1 0.6 subtract_add_fusion
  46.7 24.4 %all-gather.5.cloned.1.call-done = bf16[1024,576]{0,1:T(8,128)(2,1)} async-done(((bf16[128,576]{0,1:T(8,128)(2,1)}), bf16[1024,576]{0,1:T(8,128)(2,1)}) %all-gather.5.cloned.1.call-update) | async-done | bytes 1179664 | tf_op jit(solution)/shard_map/all_gather | solution.py:230
  71.2 1.2 pad_dynamic-slice_fusion.1
  72.4 0.0 copy-start
  72.4 1.4 copy.12.latent
  73.8 0.0 copy-done
  73.8 1.1 fusion.latent_t
  74.9 49.6 %all-gather.7.cloned.1.call-done.w = bf16[2,512,2048]{2,1,0:T(8,128)(2,1)} async-done(((bf16[2,128,2048]{2,1,0:T(8,128)(2,1)}), bf16[2,512,2048]{2,1,0:T(8,128)(2,1)}) %all-gather.7.cloned.1.call-update) | async-done | bytes 4194320 | tf_op jit(solution)/shard_map/all_gather | solution.py:234
  124.6 99.5 %shard_map.76 = (bf16[128,12288]{1,0:T(8,128)(2,1)}, bf16[2,512,2048]{2,1,0:T(8,128)(2,1)}, f32[896,576]{1,0:T(8,128)}) custom-call(bf16[128,12288]{1,0:T(8,128)(2,1)} %query.1, bf16[128,8192]{1,0:T(8,128)(2,1)} %d_attn.1, bf16[896,576]{1,0:T(8,128)(2,1)} %copy.12.latent, bf16[512,896]{1,0:T(8,128)(2,1)} %fusion.latent_t, ...), custom_call_target="tpu_custom_call" | custom-call | tf_op jit(solution)/shard_map/pallas_call | solution.py:246
  224.0 0.0 copy-start.2
  224.1 0.0 reduce-scatter.6.cloned.1.call-update
  224.1 0.0 reduce-scatter.10.cloned.1.call-start
  224.1 1.6 copy-done.2
  225.7 0.1 convert_element_type.12
  225.8 1.1 copy.13
  226.9 0.1 broadcast_in_dim.13
  227.0 0.2 constant_dynamic-update-slice_fusion
  227.2 0.1 slice.8
  227.4 1.4 copy.14
  228.8 0.0 reduce-scatter.10.cloned.1.call-update
  228.8 0.0 reduce-scatter.8.cloned.1.call-start
  228.9 48.6 %reduce-scatter.6.cloned.1.call-done = bf16[2,128,2048]{2,1,0:T(8,128)(2,1)} async-done(((bf16[2,512,2048]{2,1,0:T(8,128)(2,1)}), bf16[2,128,2048]{2,1,0:T(8,128)(2,1)}) %reduce-scatter.6.cloned.1.call-update) | async-done | bytes 1048592 | tf_op jit(solution)/shard_map/reduce_scatter | solution.py:273
  277.5 0.0 copy-start.1
  277.5 0.0 reduce-scatter.8.cloned.1.call-update
  277.5 36.1 %reduce-scatter.10.cloned.1.call-done = bf16[128,576]{1,0:T(8,128)(2,1)} async-done(((bf16[1024,576]{1,0:T(8,128)(2,1)}), bf16[128,576]{1,0:T(8,128)(2,1)}) %reduce-scatter.10.cloned.1.call-update) | async-done | bytes 147472
  313.6 1.1 copy.15
  314.7 0.7 convert_element_type.13
  315.4 31.0 %reduce-scatter.8.cloned.1.call-done = bf16[1,128,2048]{2,1,0:T(8,128)(2,1)} async-done(((bf16[2,128,2048]{2,1,0:T(8,128)(2,1)}), bf16[1,128,2048]{2,1,0:T(8,128)(2,1)}) %reduce-scatter.8.cloned.1.call-update) | async-done | bytes 524304 | tf_op jit(solution)/shard_map/reduce_scatter | solution.py:274
  346.5 2.1 bitcast_convert_fusion
  348.6 0.0 copy-done.1
  348.6 1.7 copy.18
  (1 shorter events, 0.0 us)
Async XLA Ops:
  7.2 38.7 %copy-start.3 = (s32[1,5]{1,0:T(1,128)S(1)}, s32[1,5]{1,0:T(1,128)}, u32[]{:S(2)}) copy-start(s32[1,5]{1,0:T(1,128)} %param.9) | copy-start | bytes 64
  7.2 38.6 %all-gather.9.cloned.1.call-start = ((), (), s32[]{:S(2)}) async-start(), calls=%async_computation.7 | async-start | bytes 1572864 | tf_op jit(solution)/shard_map/all_gather | solution.py:233
  7.9 63.3 %all-gather.5.cloned.1.call-start = ((), (), s32[]{:S(2)}) async-start(), calls=%async_computation.3 | async-start | bytes 1327104 | tf_op jit(solution)/shard_map/all_gather | solution.py:230
  8.7 115.9 %all-gather.7.cloned.1.call-start = ((), (), s32[]{:S(2)}) async-start(), calls=%async_computation.4 | async-start | bytes 5242880 | tf_op jit(solution)/shard_map/all_gather | solution.py:234
  45.8 231.7 %reduce-scatter.6.cloned.1.call-start = ((), (), s32[]{:S(2)}) async-start(), calls=%async_computation.5 | async-start | bytes 5242880 | tf_op jit(solution)/shard_map/reduce_scatter | solution.py:273
  72.4 1.5 copy-start
  224.0 1.6 copy-start.2
  224.1 89.6 %reduce-scatter.10.cloned.1.call-start = ((), (), s32[]{:S(2)}) async-start(), calls=%async_computation.8 | async-start | bytes 1474560
  228.8 117.6 %reduce-scatter.8.cloned.1.call-start = ((), (), s32[]{:S(2)}) async-start(), calls=%async_computation.6 | async-start | bytes 1572864 | tf_op jit(solution)/shard_map/reduce_scatter | solution.py:274
  277.5 71.1 %copy-start.1 = (bf16[128,12288]{1,0:T(8,128)(2,1)S(1)}, bf16[128,12288]{1,0:T(8,128)(2,1)}, u32[]{:S(2)}) copy-start(bf16[128,12288]{1,0:T(8,128)(2,1)} %get-tuple-element.12) | copy-start | bytes 9437188
Sparse Core Ops, SparseCore 0:
  9.6 36.1 all-gather.8
  47.3 23.7 all-gather.4
  73.0 51.4 all-gather.6
  224.2 53.2 reduce-scatter.5
  280.3 33.2 reduce-scatter.9
  315.8 30.5 reduce-scatter.7

commit v2 on v1

v2 whole, which is shorter than its diff:
```python
import functools
import math

import jax
import jax.numpy as jnp
from jax import lax
from jax.experimental import pallas as pl
from jax.experimental.pallas import tpu as pltpu
from jax.sharding import PartitionSpec as P

NOPE = 128
ROPE = 64
VDIM = 128
KV_RANK = 512
DOC_MAX = 384
QB = 128
MEMBERS = 4
AHEAD = 3
LAG = 2
MESH = pl.DeviceIdType.MESH

masked_score = -1e30
NN = (((1,), (0,)), ((), ()))
NT = (((1,), (1,)), ((), ()))
TN = (((0,), (0,)), ((), ()))


def dot(a, b, dims):
    return lax.dot_general(a, b, dims, preferred_element_type=jnp.float32)


def kernel(
    cfg,
    query,
    d_attn,
    latent,
    w_kv,
    starts,
    d_query,
    d_latent,
    d_w,
    q_buf,
    o_buf,
    dq_buf,
    w_buf,
    lat_buf,
    lat_t,
    keys,
    vals,
    dk_acc,
    dv_acc,
    dkv,
    dlat_acc,
    rope_acc,
    dw_part,
    dw_got,
    dw_mid,
    dw_fin,
    dl_part,
    dl_got,
    dl_mid,
    dl_fin,
    q_send,
    q_recv,
    o_send,
    o_recv,
    dq_send,
    dq_recv,
    w_send,
    w_recv,
    px_send,
    px_recv,
    dw_send,
    dw_recv,
    dz_send,
    dz_recv,
    lat_send,
    lat_recv,
    dl_send,
    dl_recv,
    one_send,
    one_recv,
):
    members, parts, pairs, groups = cfg
    chunks = parts * pairs
    dp = lax.axis_index("dp")
    head = lax.axis_index("head")
    part = head // members
    me = lax.rem(head, members)
    own = query.shape[0]
    held = members * own
    pad = held - DOC_MAX
    window = DOC_MAX + held
    depth = w_kv.shape[0]
    qw = 2 * (NOPE + ROPE)
    ow = 2 * VDIM
    cw = 2 * (NOPE + VDIM)
    scale = 1.0 / math.sqrt(NOPE + ROPE)
    to_exp2 = scale * math.log2(math.e)
    f32, bf16 = jnp.float32, jnp.bfloat16

    def other(k):
        return lax.rem(me + k, members)

    def peer(k):
        return (dp, part * members + other(k))

    def across(r):
        return (dp, lax.rem(part + r, parts) * members + me)

    def beside(k):
        return (lax.rem(dp + k, groups), head)

    def rows_of(index, count):
        return pl.ds(pl.multiple_of(index * count, count), count)

    def place(c):
        return lax.rem(part + c // pairs, parts), lax.rem(c, pairs)

    def pair_index(member, c):
        p, j = place(c)
        return (member + members * p) * pairs + j

    def remote(src, dst, send, recv, device):
        return pltpu.make_async_remote_copy(
            src_ref=src,
            dst_ref=dst,
            send_sem=send,
            recv_sem=recv,
            device_id=device,
            device_id_type=MESH,
        )

    def move(src, dst, send, recv, c, k):
        if k == 0:
            return pltpu.make_async_copy(src, dst, send.at[c, 0])
        return remote(src, dst, send.at[c, k], recv.at[c, k], peer(k))

    def q_copy(c, k):
        col = pl.multiple_of(pair_index(other(k), c) * qw, 128)
        dst = q_buf.at[c, rows_of(me, own)]
        return move(query.at[:, pl.ds(col, qw)], dst, q_send, q_recv, c, k)

    def o_copy(c, k):
        col = pl.multiple_of(pair_index(other(k), c) * ow, 128)
        dst = o_buf.at[c, rows_of(me, own)]
        return move(d_attn.at[:, pl.ds(col, ow)], dst, o_send, o_recv, c, k)

    def dq_copy(c, k):
        col = pl.multiple_of(pair_index(me, c) * qw, 128)
        src = dq_buf.at[c, rows_of(other(k), own)]
        return move(src, d_query.at[:, pl.ds(col, qw)], dq_send, dq_recv, c, k)

    def w_columns(c):
        return pl.ds(pl.multiple_of(lax.rem(c, pairs) * cw, cw), cw)

    def w_own(c):
        dst = w_buf.at[c, rows_of(dp, depth)]
        return pltpu.make_async_copy(w_kv.at[:, w_columns(c)], dst, px_send.at[c])

    def w_cross(c):
        dst = w_buf.at[c, rows_of(dp, depth)]
        device = across(parts - c // pairs)
        return remote(w_kv.at[:, w_columns(c)], dst, px_send.at[c], px_recv.at[c], device)

    def w_copy(c, k):
        block = w_buf.at[c, rows_of(dp, depth)]
        return remote(block, block, w_send.at[c, k], w_recv.at[c, k], beside(k))

    def dw_copy(c, k):
        src = dw_part.at[c, rows_of(lax.rem(dp + k, groups), depth)]
        return remote(src, dw_got.at[c, k], dw_send.at[c, k], dw_recv.at[c, k], beside(k))

    def dz_copy(c):
        device = across(c // pairs)
        return remote(dw_mid.at[c], dw_fin.at[c], dz_send.at[c], dz_recv.at[c], device)

    def lat_copy(side, k):
        block = lat_buf.at[side, rows_of(me, own)]
        if k == 0:
            return pltpu.make_async_copy(latent, block, lat_send.at[side, 0])
        src = latent if side == 1 else block
        return remote(src, block, lat_send.at[side, k], lat_recv.at[side, k], peer(k))

    def lat_cross():
        dst = lat_buf.at[0, rows_of(me, own)]
        return remote(latent, dst, one_send.at[0], one_recv.at[0], across(1))

    def dl_copy(k):
        src = dl_part.at[other(k)]
        return remote(src, dl_got.at[k], dl_send.at[k], dl_recv.at[k], peer(k))

    def dl_cross():
        return remote(dl_mid, dl_fin, one_send.at[1], one_recv.at[1], across(parts - 1))

    def launch(c):
        for k in list(range(1, members)) + [0]:
            q_copy(c, k).start()
            o_copy(c, k).start()

        @pl.when(c < pairs)
        def _():
            w_own(c).wait()

        @pl.when(c >= pairs)
        def _():
            w_cross(c).wait_recv()

        @pl.loop(1, groups)
        def _(k):
            w_copy(c, k).start()

    barrier = pltpu.get_barrier_semaphore()

    def greet(device):
        pl.semaphore_signal(barrier, inc=1, device_id=device, device_id_type=MESH)

    for k in range(1, members):
        greet(peer(k))
    for r in range(1, parts):
        greet(across(r))

    @pl.loop(1, groups)
    def _(k):
        greet(beside(k))

    pl.semaphore_wait(barrier, members + parts + groups - 3)

    lat_cross().start()
    for k in list(range(1, members)) + [0]:
        lat_copy(1, k).start()

    @pl.loop(0, pairs)
    def _(c):
        w_own(c).start()

    @pl.loop(pairs, chunks)
    def _(c):
        w_cross(c).start()

    launch(jnp.int32(0))
    lat_cross().wait_recv()
    for k in range(1, members):
        lat_copy(0, k).start()

    @pl.loop(1, AHEAD)
    def _(c):
        launch(c)

    dlat_acc[...] = jnp.zeros_like(dlat_acc)
    rope_acc[...] = jnp.zeros_like(rope_acc)
    lat_copy(1, 0).wait()
    for k in range(1, members):
        lat_copy(1, k).wait_recv()
        lat_copy(0, k).wait_recv()

    half = NOPE // 2
    lane = lax.broadcasted_iota(jnp.int32, (window, NOPE), 1)
    low_lane = lane < half
    near = jnp.concatenate([lat_buf[0, pad:], lat_buf[1]], axis=0)
    lat_t[...] = jnp.transpose(near[:, :KV_RANK])
    rope = near[:, KV_RANK:].astype(f32)
    empty = jnp.zeros_like(rope)
    keys[0, :, NOPE:] = jnp.concatenate([rope, empty], axis=1).astype(bf16)
    keys[2, :, NOPE:] = jnp.concatenate([empty, rope], axis=1).astype(bf16)

    def settle(c):
        @pl.loop(1, groups)
        def _(k):
            dw_copy(c, k).wait_recv()

        total = dw_part[c, rows_of(dp, depth)].astype(f32)
        for k in range(1, groups):
            total += dw_got[c, k].astype(f32)

        @pl.when(c < pairs)
        def _():
            d_w[:, w_columns(c)] = total

        @pl.when(c >= pairs)
        def _():
            dw_mid[c] = total.astype(bf16)
            dz_copy(c).start()

    @pl.loop(0, chunks)
    def _(c):
        @pl.when(c + AHEAD < chunks)
        def _():
            launch(c + AHEAD)

        @pl.when(c >= LAG)
        def _():
            settle(c - LAG)

        @pl.loop(1, groups)
        def _(k):
            w_copy(c, k).wait_recv()

        weight = w_buf.at[c]
        split = DOC_MAX
        for side, rows in ((0, slice(0, split)), (1, slice(split, window))):
            lat = lat_buf[0, pad:, :KV_RANK] if side == 0 else lat_buf[1, :, :KV_RANK]
            kv = dot(lat, weight[...], NN)
            keys[0, rows, :NOPE] = kv[:, :NOPE].astype(bf16)
            vals[0, rows] = kv[:, NOPE : 2 * NOPE].astype(bf16)
            rolled = pltpu.roll(kv[:, 2 * NOPE : 3 * NOPE], half, 1)
            lower = low_lane[rows]
            keys[1, rows, :NOPE] = jnp.where(lower, 0.0, rolled).astype(bf16)
            keys[1, rows, NOPE:] = jnp.where(
                lower, rolled, keys[2, rows, NOPE:].astype(f32)
            ).astype(bf16)
            vals[1, rows] = kv[:, 3 * NOPE :].astype(bf16)
        for k in range(members):
            if k == 0:
                q_copy(c, k).wait()
                o_copy(c, k).wait()
            else:
                q_copy(c, k).wait_recv()
                o_copy(c, k).wait_recv()
        dk_acc[...] = jnp.zeros_like(dk_acc)
        dv_acc[...] = jnp.zeros_like(dv_acc)
        for b in range(held // QB):
            rows = slice(b * QB, (b + 1) * QB)
            span = slice(b * QB, b * QB + DOC_MAX + QB)
            shape = (DOC_MAX + QB, QB)
            key_pos = lax.broadcasted_iota(jnp.int32, shape, 0) + b * QB
            query_pos = lax.broadcasted_iota(jnp.int32, shape, 1) + (DOC_MAX + b * QB)
            allowed = (key_pos <= query_pos) & (key_pos >= starts[:, rows])
            grads = []
            for h in range(2):
                q = q_buf[c, rows, h * NOPE : h * NOPE + 2 * NOPE]
                o = o_buf[c, rows, h * VDIM : (h + 1) * VDIM]
                key = keys[h, span]
                s = dot(key, q, NT)
                s = jnp.where(allowed, s, masked_score)
                top = jnp.max(s, axis=0, keepdims=True)
                e = jnp.exp2((s - top) * to_exp2)
                probs = e * (1.0 / jnp.sum(e, axis=0, keepdims=True))
                low = probs.astype(bf16)
                dprob = dot(vals[h, span], o, NT)
                delta = jnp.sum(low.astype(f32) * dprob, axis=0, keepdims=True)
                ds = (probs * (dprob - delta)).astype(bf16)
                dv_acc[h, span] += dot(low, o, NN)
                dk_acc[h, span] += dot(ds, q, NN)
                grads.append(dot(ds, key, TN) * scale)
            a, z = grads
            dq_buf[c, rows, :NOPE] = a[:, :NOPE].astype(bf16)
            dq_buf[c, rows, NOPE : 2 * NOPE] = (a[:, NOPE:] + z[:, :NOPE]).astype(bf16)
            dq_buf[c, rows, 2 * NOPE :] = z[:, NOPE:].astype(bf16)
        for k in list(range(1, members)) + [0]:
            dq_copy(c, k).start()
        dkv[:, :NOPE] = (dk_acc[0, :, :NOPE] * scale).astype(bf16)
        dkv[:, NOPE : 2 * NOPE] = dv_acc[0].astype(bf16)
        turned_a = pltpu.roll(dk_acc[1, :, :NOPE], half, 1)
        turned_b = pltpu.roll(dk_acc[1, :, NOPE:], half, 1)
        dkv[:, 2 * NOPE : 3 * NOPE] = (jnp.where(low_lane, turned_a, turned_b) * scale).astype(bf16)
        dkv[:, 3 * NOPE :] = dv_acc[1].astype(bf16)
        dw_part[c] = dot(lat_t[...], dkv[...], NN).astype(bf16)

        @pl.loop(1, groups)
        def _(k):
            dw_copy(c, k).start()

        rope_acc[...] += dk_acc[0, :, NOPE:] + turned_b
        dlat_acc[...] += dot(dkv[...], weight[...], NT)

    for index in range(2 * members):
        side, m, first = index // members, index % members, index * own - pad
        if first < 0:
            dl_part[m, side] = jnp.zeros_like(dl_part[m, side])
        else:
            rows = slice(first, first + own)
            dl_part[m, side, :, :KV_RANK] = dlat_acc[rows].astype(bf16)
            dl_part[m, side, :, KV_RANK:] = (rope_acc[rows, :ROPE] * scale).astype(bf16)
    for k in range(1, members):
        dl_copy(k).start()

    @pl.loop(chunks - LAG, chunks)
    def _(c):
        settle(c)

    for k in range(1, members):
        dl_copy(k).wait_recv()
    back = dl_part[me, 0].astype(f32)
    kept = dl_part[me, 1].astype(f32)
    for k in range(1, members):
        back += dl_got[k, 0].astype(f32)
        kept += dl_got[k, 1].astype(f32)
    dl_mid[...] = back.astype(bf16)
    dl_cross().start()

    @pl.loop(pairs, chunks)
    def _(c):
        dz_copy(c).wait()
        d_w[:, w_columns(c)] += dw_fin[c].astype(f32)

    dl_cross().wait()
    d_latent[...] = kept + dl_fin[...].astype(f32)

    lat_cross().wait_send()
    for k in range(1, members):
        lat_copy(0, k).wait_send()
        lat_copy(1, k).wait_send()
        dl_copy(k).wait_send()

    @pl.loop(pairs, chunks)
    def _(c):
        w_cross(c).wait_send()

    @pl.loop(0, chunks)
    def _(c):
        for k in range(members):
            if k == 0:
                dq_copy(c, k).wait()
            else:
                q_copy(c, k).wait_send()
                o_copy(c, k).wait_send()
                dq_copy(c, k).wait()

        @pl.loop(1, groups)
        def _(k):
            w_copy(c, k).wait_send()
            dw_copy(c, k).wait_send()


def local(query, latent, d_attn, w_kv, doc_lengths):
    group = lax.axis_size("head")
    groups = lax.axis_size("dp")
    head = lax.axis_index("head")
    own, wide = latent.shape
    members = min(MEMBERS, group // 2)
    parts = group // members
    held = members * own
    depth = w_kv.shape[0]
    pairs = w_kv.shape[1] // (2 * (NOPE + VDIM))
    chunks = parts * pairs
    window = DOC_MAX + held
    first = (head // members) * held

    ends = jnp.cumsum(doc_lengths[0])
    positions = first + jnp.arange(held, dtype=jnp.int32)
    starts = jnp.max(jnp.where(ends[None, :] <= positions[:, None], ends[None, :], 0), axis=1)
    starts = (starts - first + DOC_MAX).astype(jnp.int32)[None, :]

    hbm = pl.BlockSpec(memory_space=pl.ANY)
    vmem = pl.BlockSpec(memory_space=pltpu.VMEM)
    bf16, f32 = jnp.bfloat16, jnp.float32
    qw, ow, cw = 2 * (NOPE + ROPE), 2 * VDIM, 2 * (NOPE + VDIM)
    by_member = pltpu.SemaphoreType.DMA((chunks, members))
    by_group = pltpu.SemaphoreType.DMA((chunks, groups))
    by_chunk = pltpu.SemaphoreType.DMA((chunks,))
    few = pltpu.SemaphoreType.DMA((2, members))
    return pl.pallas_call(
        functools.partial(kernel, (members, parts, pairs, groups)),
        out_shape=(
            jax.ShapeDtypeStruct(query.shape, bf16),
            jax.ShapeDtypeStruct(latent.shape, f32),
            jax.ShapeDtypeStruct(w_kv.shape, f32),
        ),
        in_specs=[hbm, hbm, hbm, hbm, vmem],
        out_specs=(hbm, vmem, vmem),
        scratch_shapes=[
            pltpu.VMEM((chunks, held, qw), bf16),
            pltpu.VMEM((chunks, held, ow), bf16),
            pltpu.VMEM((chunks, held, qw), bf16),
            pltpu.VMEM((chunks, KV_RANK, cw), bf16),
            pltpu.VMEM((2, held, wide), bf16),
            pltpu.VMEM((KV_RANK, window), bf16),
            pltpu.VMEM((3, window, 2 * NOPE), bf16),
            pltpu.VMEM((2, window, VDIM), bf16),
            pltpu.VMEM((2, window, 2 * NOPE), f32),
            pltpu.VMEM((2, window, VDIM), f32),
            pltpu.VMEM((window, cw), bf16),
            pltpu.VMEM((window, KV_RANK), f32),
            pltpu.VMEM((window, NOPE), f32),
            pltpu.VMEM((chunks, KV_RANK, cw), bf16),
            pltpu.VMEM((chunks, groups, depth, cw), bf16),
            pltpu.VMEM((chunks, depth, cw), bf16),
            pltpu.VMEM((chunks, depth, cw), bf16),
            pltpu.VMEM((members, 2, own, wide), bf16),
            pltpu.VMEM((members, 2, own, wide), bf16),
            pltpu.VMEM((own, wide), bf16),
            pltpu.VMEM((own, wide), bf16),
        ]
        + [by_member] * 6
        + [by_group] * 2
        + [by_chunk] * 2
        + [by_group] * 2
        + [by_chunk] * 2
        + [few] * 2
        + [pltpu.SemaphoreType.DMA((members,))] * 2
        + [pltpu.SemaphoreType.DMA((2,))] * 2,
        compiler_params=pltpu.CompilerParams(
            collective_id=0, has_side_effects=True, vmem_limit_bytes=56 * 2**20
        ),
    )(query, d_attn, latent, w_kv, starts)


def solution(mesh):
    placed = (
        P(("dp", "head"), None),
        P(("dp", "head"), None),
        P(("dp", "head"), None),
        P("dp", "head"),
        P("dp", None),
    )
    return jax.shard_map(
        local,
        mesh=mesh,
        in_specs=placed,
        out_specs=(P(("dp", "head"), None), P(("dp", "head"), None), P("dp", "head")),
        check_vma=False,
    )
```

time: 357 us -> 173 us (0.48)
  the two profiles are of different devices: /device:TPU:0 before, /device:TPU:1 now
where the time goes in v2:
time: 173 us
  Pallas kernels  162 us (94%)
  local copies, waits for them, and re-layouts  8.44 us (5%)
    pallas_call x1, Pallas kernels, local(): pl.pallas_call(functools.partial(kernel, (members, parts, pairs, groups))...  162 us
    unnamed x5, local copies, waits for them, and re-layouts  6.61 us

profile of v2, /device:TPU:1, one launch (start us, length us, event | category | flops | bytes accessed | tf_op | source)
XLA Modules:
  0.0 173.0 jit_solution(18421982758962138036)
XLA Ops:
  0.6 0.8 reduce-window.8
  1.5 0.1 select_reduce_fusion
  1.6 0.6 subtract_add_fusion
  2.1 1.7 copy.10.latent
  3.9 162.4 %shard_map.76 = (bf16[128,12288]{1,0:T(8,128)(2,1)}, f32[128,576]{1,0:T(8,128)}, f32[128,2048]{1,0:T(8,128)}) custom-call(bf16[128,12288]{1,0:T(8,128)(2,1)} %query.1, bf16[128,8192]{1,0:T(8,128)(2,1)} %d_attn.1, bf16[128,576]{1,0:T(8,128)(2,1)} %copy.10.latent, bf16[128,2048]{1,0:T(8,128)(2,1)} %w_kv.1, s32[1,512]{1,0:T(1,128)} %bitcast.3), custom_call_target="tpu_custom_call" | custom-call | tf_op jit(solution)/shard_map/pallas_call | solution.py:453
  166.2 1.8 %copy.11 = f32[128,576]{0,1:T(8,128)} copy(f32[128,576]{1,0:T(8,128)} %get-tuple-element.7) | data formatting | bytes 589824 | tf_op jit(solution)/shard_map/pallas_call | solution.py:453
  168.1 0.0 copy-start
  168.1 3.9 %copy.14 = bf16[128,12288]{1,0:T(8,128)(2,1)} copy(bf16[128,12288]{1,0:T(8,128)(2,1)} %get-tuple-element.12) | data formatting | bytes 6291456
  172.0 0.0 copy-done
  172.0 1.0 copy.15
  (1 shorter events, 0.0 us)
Async XLA Ops:
  168.1 3.9 %copy-start = (f32[128,2048]{1,0:T(8,128)S(1)}, f32[128,2048]{1,0:T(8,128)}, u32[]{:S(2)}) copy-start(f32[128,2048]{1,0:T(8,128)} %get-tuple-element.14) | copy-start | bytes 3145732

commit v3 on v2

--- a/solution.py
+++ b/solution.py
@@ -13,7 +13,7 @@
 VDIM = 128
 KV_RANK = 512
 DOC_MAX = 384
-QB = 128
+QB = 256
 MEMBERS = 4
 AHEAD = 3
 LAG = 2
@@ -57,6 +57,7 @@
     dw_mid,
     dw_fin,
     dl_part,
+    dl_sum,
     dl_got,
     dl_mid,
     dl_fin,
@@ -175,20 +176,31 @@
         device = across(c // pairs)
         return remote(dw_mid.at[c], dw_fin.at[c], dz_send.at[c], dz_recv.at[c], device)
 
+    twin = me + 1 - 2 * lax.rem(me, 2)
+    facing = lax.rem(me + 2, members)
+    to_twin = (dp, part * members + twin)
+    to_facing = (dp, part * members + facing)
+
     def lat_copy(side, k):
         block = lat_buf.at[side, rows_of(me, own)]
         if k == 0:
             return pltpu.make_async_copy(latent, block, lat_send.at[side, 0])
         src = latent if side == 1 else block
-        return remote(src, block, lat_send.at[side, k], lat_recv.at[side, k], peer(k))
+        if k == 3:
+            src = block = lat_buf.at[side, rows_of(facing, own)]
+        device = to_facing if k == 2 else to_twin
+        return remote(src, block, lat_send.at[side, k], lat_recv.at[side, k], device)
 
     def lat_cross():
         dst = lat_buf.at[0, rows_of(me, own)]
         return remote(latent, dst, one_send.at[0], one_recv.at[0], across(1))
 
     def dl_copy(k):
-        src = dl_part.at[other(k)]
-        return remote(src, dl_got.at[k], dl_send.at[k], dl_recv.at[k], peer(k))
+        if k == 2:
+            src, device = dl_sum, to_facing
+        else:
+            src, device = dl_part.at[lax.rem(twin + 2 * k, members)], to_twin
+        return remote(src, dl_got.at[k], dl_send.at[k], dl_recv.at[k], device)
 
     def dl_cross():
         return remote(dl_mid, dl_fin, one_send.at[1], one_recv.at[1], across(parts - 1))
@@ -227,30 +239,36 @@
     pl.semaphore_wait(barrier, members + parts + groups - 3)
 
     lat_cross().start()
-    for k in list(range(1, members)) + [0]:
+    for k in (2, 1, 0):
         lat_copy(1, k).start()
 
     @pl.loop(0, pairs)
     def _(c):
         w_own(c).start()
 
+    launch(jnp.int32(0))
+    lat_copy(1, 2).wait_recv()
+    lat_copy(1, 3).start()
+    lat_cross().wait_recv()
+    for k in (2, 1):
+        lat_copy(0, k).start()
+    launch(jnp.int32(1))
+
     @pl.loop(pairs, chunks)
     def _(c):
         w_cross(c).start()
 
-    launch(jnp.int32(0))
-    lat_cross().wait_recv()
-    for k in range(1, members):
-        lat_copy(0, k).start()
-
-    @pl.loop(1, AHEAD)
+    lat_copy(0, 2).wait_recv()
+    lat_copy(0, 3).start()
+
+    @pl.loop(2, AHEAD)
     def _(c):
         launch(c)
 
     dlat_acc[...] = jnp.zeros_like(dlat_acc)
     rope_acc[...] = jnp.zeros_like(rope_acc)
     lat_copy(1, 0).wait()
-    for k in range(1, members):
+    for k in (1, 3):
         lat_copy(1, k).wait_recv()
         lat_copy(0, k).wait_recv()
 
@@ -372,20 +390,22 @@
             rows = slice(first, first + own)
             dl_part[m, side, :, :KV_RANK] = dlat_acc[rows].astype(bf16)
             dl_part[m, side, :, KV_RANK:] = (rope_acc[rows, :ROPE] * scale).astype(bf16)
-    for k in range(1, members):
+    for k in (1, 0):
         dl_copy(k).start()
+    dl_copy(1).wait_recv()
+    dl_sum[...] = (dl_part[facing].astype(f32) + dl_got[1].astype(f32)).astype(bf16)
+    dl_copy(2).start()
 
     @pl.loop(chunks - LAG, chunks)
     def _(c):
         settle(c)
 
-    for k in range(1, members):
+    for k in (0, 2):
         dl_copy(k).wait_recv()
-    back = dl_part[me, 0].astype(f32)
-    kept = dl_part[me, 1].astype(f32)
-    for k in range(1, members):
-        back += dl_got[k, 0].astype(f32)
-        kept += dl_got[k, 1].astype(f32)
+    back, kept = [
+        dl_part[me, side].astype(f32) + dl_got[0, side].astype(f32) + dl_got[2, side].astype(f32)
+        for side in range(2)
+    ]
     dl_mid[...] = back.astype(bf16)
     dl_cross().start()
 
@@ -401,7 +421,7 @@
     for k in range(1, members):
         lat_copy(0, k).wait_send()
         lat_copy(1, k).wait_send()
-        dl_copy(k).wait_send()
+        dl_copy(k - 1).wait_send()
 
     @pl.loop(pairs, chunks)
     def _(c):
@@ -478,7 +498,8 @@
             pltpu.VMEM((chunks, depth, cw), bf16),
             pltpu.VMEM((chunks, depth, cw), bf16),
             pltpu.VMEM((members, 2, own, wide), bf16),
-            pltpu.VMEM((members, 2, own, wide), bf16),
+            pltpu.VMEM((2, own, wide), bf16),
+            pltpu.VMEM((3, 2, own, wide), bf16),
             pltpu.VMEM((own, wide), bf16),
             pltpu.VMEM((own, wide), bf16),
         ]

time: 173 us -> 159 us (0.919)
  the two profiles are of different devices: /device:TPU:1 before, /device:TPU:0 now
where the time goes in v3:
time: 159 us; the launch traced here: 158 us
  Pallas kernels  147 us (92%)
  local copies, waits for them, and re-layouts  8.44 us (5%)
    pallas_call x1, Pallas kernels, local(): pl.pallas_call(functools.partial(kernel, (members, parts, pairs, groups))...  147 us
    unnamed x5, local copies, waits for them, and re-layouts  6.61 us

profile of v3, /device:TPU:0, one launch (start us, length us, event | category | flops | bytes accessed | tf_op | source)
XLA Modules:
  0.0 157.8 jit_solution(10638399044031527361)
XLA Ops:
  0.6 0.8 reduce-window.8
  1.5 0.1 select_reduce_fusion
  1.6 0.6 subtract_add_fusion
  2.1 1.7 %copy.10.latent = bf16[128,576]{1,0:T(8,128)(2,1)} copy(bf16[128,576]{0,1:T(8,128)(2,1)} %param.6) | data formatting | bytes 294912 | tf_op args[1]
  3.9 147.2 %shard_map.76 = (bf16[128,12288]{1,0:T(8,128)(2,1)}, f32[128,576]{1,0:T(8,128)}, f32[128,2048]{1,0:T(8,128)}) custom-call(bf16[128,12288]{1,0:T(8,128)(2,1)} %query.1, bf16[128,8192]{1,0:T(8,128)(2,1)} %d_attn.1, bf16[128,576]{1,0:T(8,128)(2,1)} %copy.10.latent, bf16[128,2048]{1,0:T(8,128)(2,1)} %w_kv.1, s32[1,512]{1,0:T(1,128)} %bitcast.3), custom_call_target="tpu_custom_call" | custom-call | tf_op jit(solution)/shard_map/pallas_call | solution.py:473
  151.0 1.8 %copy.11 = f32[128,576]{0,1:T(8,128)} copy(f32[128,576]{1,0:T(8,128)} %get-tuple-element.7) | data formatting | bytes 589824 | tf_op jit(solution)/shard_map/pallas_call | solution.py:473
  152.9 0.0 copy-start
  152.9 3.9 %copy.14 = bf16[128,12288]{1,0:T(8,128)(2,1)} copy(bf16[128,12288]{1,0:T(8,128)(2,1)} %get-tuple-element.12) | data formatting | bytes 6291456
  156.8 0.0 copy-done
  156.8 1.0 copy.15
  (1 shorter events, 0.0 us)
Async XLA Ops:
  152.9 3.9 %copy-start = (f32[128,2048]{1,0:T(8,128)S(1)}, f32[128,2048]{1,0:T(8,128)}, u32[]{:S(2)}) copy-start(f32[128,2048]{1,0:T(8,128)} %get-tuple-element.14) | copy-start | bytes 3145732
